TPU v7x, 32 devices: a whole 2x2x4 slice. The times are simulated.
32 devices in a mesh: slab: 8 (over z, x), pencil: 4 (over y, core).
Axes of the slice: x: 2, y: 2, z: 4, core: 2. Of those that a mesh axis runs over, the one named last changes fastest.
Arguments:
- vorticity: float32 [3, 64, 128, 256], P(None, 'slab', 'pencil')
- velocity: float32 [3, 64, 128, 256], P(None, 'slab', 'pencil'), may hold values from -6 to 6
- viscosity: float32 [64, 128, 256], P('slab', 'pencil'), may hold values from 0.02 to 0.4
- tile_weights: float32 [1024, 3, 128], P(('slab', 'pencil')), may hold values from -6 to 6
- tile_cells: int32 [1024, 128], P(('slab', 'pencil')), may hold values from 0 to 65535
- tile_dest: int32 [1024, 1], P(('slab', 'pencil')), may hold values from 0 to 7; in each aligned block of 32 rows (0 to 31, 32 to 63, ...) at most 8 rows name the same one
- tile_count: int32 [32], P(('slab', 'pencil')), may hold values from 8 to 32, as said below
Outputs:
- vorticity_out: float32 [3, 64, 128, 256], P(None, 'slab', 'pencil')
- far_velocity: float32 [3, 8, 4, 16], P(None, 'slab', 'pencil')
Inputs may be any that keep to these rules, and one draw needn't show every extreme that they name: Tiles of device (s, p) go to device (tile_dest, p). Among the 32 tiles of one device, at most 8 name one slab, a bound that some block reaches. The live tiles of a device are its first tile_count ones; some device has all 32 live.
All inputs are finite; a program needn't handle non-finite values.
Results may differ from a plain program's by a relative error of at most 0.0003.
Values sent between devices are 32-bit elements; how exact they have to be, the bound alone decides.
No kernel may reach another device: no remote copies, remote signals or barrier semaphores. Data moves between devices by JAX's collectives and lax.ppermute only.
A program may use at most 128 MiB of HBM per device.

v0:
```python
import jax
import jax.numpy as jnp
from jax import lax
from jax.sharding import PartitionSpec as P

CB = 16
NCL = 16


time_step = 0.1


def with_halo(array, sides, width):
    for axis, dim in sides:
        devices, length = (lax.axis_size(axis), array.shape[dim])
        up = [(i, (i + 1) % devices) for i in range(devices - 1)]
        down = [(j, i) for i, j in up]
        last = lax.slice_in_dim(array, length - width, length, axis=dim)
        leading = lax.slice_in_dim(array, 0, width, axis=dim)
        before = lax.ppermute(last, axis, up)
        after = lax.ppermute(leading, axis, down)
        array = jnp.concatenate([before, array, after], axis=dim)
    return array


def interior(a):
    return a[..., 1:-1, 1:-1, :]


def ahead_x(a):
    return a[..., 2:, 1:-1, :]


def behind_x(a):
    return a[..., :-2, 1:-1, :]


def ahead_y(a):
    return a[..., 1:-1, 2:, :]


def behind_y(a):
    return a[..., 1:-1, :-2, :]


def ahead_z(a):
    return jnp.roll(interior(a), -1, axis=-1)


def behind_z(a):
    return jnp.roll(interior(a), 1, axis=-1)


def advance(padded):
    vort_all = padded[0:3]
    velo_all = padded[3:6]
    visc_all = padded[6]
    stencil_pairs = ((ahead_x, behind_x), (ahead_y, behind_y), (ahead_z, behind_z))
    own_vort = interior(vort_all)
    own_visc = interior(visc_all)
    stretch = jnp.zeros_like(own_vort)
    diffuse = jnp.zeros_like(own_vort)
    for axis_num in range(3):
        forward, backward = stencil_pairs[axis_num]
        stretch = stretch + own_vort[axis_num] * (0.5 * (forward(velo_all) - backward(velo_all)))
        for neighbour in stencil_pairs[axis_num]:
            diffuse = diffuse + 0.5 * (own_visc + neighbour(visc_all)) * (
                neighbour(vort_all) - own_vort
            )
    return own_vort + time_step * (stretch + diffuse)


def centres(cols, cx, cy, cb, npencil, ncl):
    slab_idx = cols // (npencil * ncl)
    pencil_idx = cols // ncl % npencil
    level = cols % ncl
    xpos = (slab_idx * cx).astype(jnp.float32) + (cx - 1) * 0.5
    ypos = (pencil_idx * cy).astype(jnp.float32) + (cy - 1) * 0.5
    zpos = (level * cb).astype(jnp.float32) + (cb - 1) * 0.5
    return (xpos, ypos, zpos)


def far_terms(targets, sources, moments, sigma):
    high = lax.Precision.HIGHEST
    rel_x = targets[0][:, None] - sources[0][None, :]
    rel_y = targets[1][:, None] - sources[1][None, :]
    rel_z = targets[2][:, None] - sources[2][None, :]
    dist_sq = rel_x * rel_x + rel_y * rel_y + rel_z * rel_z + sigma * sigma
    inverse = lax.rsqrt(dist_sq)
    weight = inverse * inverse * inverse
    trans = moments.T
    along_x = jnp.dot(weight * rel_x, trans, precision=high)
    along_y = jnp.dot(weight * rel_y, trans, precision=high)
    along_z = jnp.dot(weight * rel_z, trans, precision=high)
    first = along_z[:, 1] - along_y[:, 2]
    second = along_x[:, 2] - along_z[:, 0]
    third = along_y[:, 0] - along_x[:, 1]
    return jnp.stack([first, second, third], 0)


def deposit(field_flat, weights, local_cells):
    values = jnp.transpose(weights, (1, 0, 2)).reshape(3, -1)
    return field_flat.at[:, local_cells.reshape(-1)].add(values)


def per_device(vorticity, velocity, viscosity, tile_weights, tile_cells, tile_dest, tile_count):
    cx_dev = vorticity.shape[1]
    cy_dev = vorticity.shape[2]
    nz_all = vorticity.shape[3]
    cells_dev = cx_dev * cy_dev * nz_all
    tiles_dev = tile_weights.shape[0]
    tile_len = tile_weights.shape[2]
    n_slab = lax.axis_size("slab")
    n_pencil = lax.axis_size("pencil")
    stacked = jnp.concatenate([vorticity, velocity, viscosity[None]], 0)
    padded = with_halo(stacked, (("slab", 1), ("pencil", 2)), 1)
    advanced = advance(padded)
    field = advanced.reshape(3, cells_dev)
    live = (jnp.arange(tiles_dev, dtype=jnp.int32) < tile_count[0]).astype(jnp.float32)
    live_weights = tile_weights * live[:, None, None]
    dest = tile_dest[:, 0]
    coded = (tile_cells + dest[:, None] * cells_dev).astype(jnp.float32)
    payload = jnp.concatenate([live_weights, coded[:, None, :]], 1)
    arrived = lax.all_gather(payload, "slab", axis=0, tiled=True)
    code_int = arrived[:, 3, :].astype(jnp.int32)
    row_target = code_int[:, 0] // cells_dev
    local_cells = code_int - row_target[:, None] * cells_dev
    keep_row = row_target == lax.axis_index("slab")
    rows_kept = 2 * tiles_dev
    position = jnp.cumsum(keep_row.astype(jnp.int32)) - 1
    position = jnp.where(keep_row, position, rows_kept)
    compact_weights = (
        jnp.zeros((rows_kept, 3, tile_len), jnp.float32)
        .at[position]
        .set(arrived[:, 0:3, :], mode="drop")
    )
    compact_cells = (
        jnp.zeros((rows_kept, tile_len), jnp.int32).at[position].set(local_cells, mode="drop")
    )
    field = deposit(field, compact_weights, compact_cells)
    vorticity_out = field.reshape(3, cx_dev, cy_dev, nz_all)
    moment = vorticity_out.reshape(3, cx_dev, cy_dev, NCL, CB).sum(axis=(1, 2, 4))
    sigma = jnp.float32(cx_dev * n_slab // 4)
    own_cols = (lax.axis_index("slab") * n_pencil + lax.axis_index("pencil")) * NCL + jnp.arange(
        NCL, dtype=jnp.int32
    )
    targets = centres(own_cols, cx_dev, cy_dev, CB, n_pencil, NCL)
    piece = lax.all_gather(moment, ("slab", "pencil"), axis=1, tiled=True)
    cols = jnp.arange(piece.shape[1], dtype=jnp.int32)
    sources = centres(cols, cx_dev, cy_dev, CB, n_pencil, NCL)
    far_local = far_terms(targets, sources, piece, sigma)
    far_velocity = far_local.reshape(3, 1, 1, NCL)
    return (vorticity_out, far_velocity)


def solution(mesh):
    in_specs = (
        P(None, "slab", "pencil", None),
        P(None, "slab", "pencil", None),
        P("slab", "pencil", None),
        P(("slab", "pencil"), None, None),
        P(("slab", "pencil"), None),
        P(("slab", "pencil"), None),
        P(("slab", "pencil")),
    )
    out_specs = (P(None, "slab", "pencil", None), P(None, "slab", "pencil", None))
    return jax.shard_map(
        per_device, mesh=mesh, in_specs=in_specs, out_specs=out_specs, check_vma=False
    )
```

profile of v0, /device:TPU:0, one launch (start us, length us, event | category | flops | bytes accessed | tf_op | source)
XLA Modules:
  0.0 259.6 jit_solution(14367739716480451195)
XLA Ops:
  0.7 2.0 pad_maximum_fusion.22
  2.7 1.3 collective-permute-start
  4.0 6.2 %collective-permute-start.1 = (f32[7,1,32,256]{3,2,1,0:T(8,128)}, f32[7,1,32,256]{3,2,1,0:T(8,128)}, u32[]{:S(2)}, u32[]{:S(2)}) collective-permute-start(f32[7,1,32,256]{3,2,1,0:T(8,128)} %get-tuple-element.16), channel_id=1, source_target_pairs={{0,4},{4,8},{8,12},{12,16},{16,20},{20,24},{24,28},{1,5},{5,9},{9,... | collective-permute-start | bytes 688136 | tf_op jit(solution)/shard_map/ppermute | solution.py:20
  10.1 3.6 %fusion.96 = (f32[3,8,32,255]{3,2,1,0:T(8,128)S(1)}, f32[3,8,32,255]{3,2,1,0:T(8,128)S(1)}, f32[3,8,32,255]{3,2,1,0:T(8,128)}, f32[3,8,32,255]{3,2,1,0:T(8,128)}) fusion(f32[3,8,32,256]{3,2,1,0:T(8,128)} %param.7, f32[3,8,32,256]{3,2,1,0:T(8,128)} %param.8), kind=kLoop, calls=%fused_computation.200 | loop fusion | bytes 6266880 | tf_op jit(solution)/shard_map/jit(_roll_static)/slice | solution.py:51
  13.7 2.7 %fusion.95 = (f32[3,8,32,1]{3,2,1,0:T(8,128)}, f32[3,8,32,1]{3,2,1,0:T(8,128)}, f32[3,8,32,1]{3,2,1,0:T(8,128)}, f32[3,8,32,1]{3,2,1,0:T(8,128)}) fusion(f32[3,8,32,256]{3,2,1,0:T(8,128)} %param.7, f32[3,8,32,256]{3,2,1,0:T(8,128)} %param.8), kind=kLoop, calls=%fused_computation.199 | loop fusion | bytes 24576 | tf_op jit(solution)/shard_map/jit(_roll_static)/slice | solution.py:51
  17.8 0.9 broadcast_multiply_fusion
  19.4 32.2 %all_gather.6 = f32[256,4,128]{2,0,1:T(8,128)S(1)} all-gather(f32[32,4,128]{2,0,1:T(8,128)S(1)} %pad_maximum_fusion.30), channel_id=1, replica_groups=mesh['slab'=8,'pencil'=4] {'slab'}, dimensions={0}, use_global_device_ids=true | all-gather | bytes 589824 | tf_op jit(solution)/shard_map/all_gather | solution.py:124
  55.1 0.8 copy.58
  55.9 1.1 fusion.31
  57.0 1.6 scatter_custom_fusion
  59.3 2.1 copy.59
  61.4 15.1 %scatter_fusion = f32[64,3,128]{2,1,0:T(4,128)S(1)} fusion(f32[64,3,128]{2,1,0:T(4,128)S(1)} %broadcast_in_dim.16, s32[256]{0:T(256)S(1)} %fusion.31, f32[256,3,128]{2,1,0:T(4,128)} %copy.59), kind=kCustom, calls=%fused_computation.1 | custom fusion | bytes 1180672 | tf_op jit(solution)/shard_map/scatter | solution.py:135
  76.5 2.7 %copy.60 = f32[8192,3]{1,0:T(8,128)} copy(f32[8192,3]{0,1:T(4,128)S(1)} %bitcast.59) | data formatting | bytes 196608 | tf_op jit(solution)/shard_map/reshape | solution.py:102
  79.3 1.2 multiply_bitcast_fusion.2
  80.5 1.5 pad_maximum_fusion.29
  82.0 1.3 collective-permute-start.2
  83.3 3.0 %collective-permute-start.3 = (f32[7,10,1,256]{3,0,2,1:T(8,128)S(1)}, f32[7,10,1,256]{3,0,2,1:T(8,128)S(1)}, u32[]{:S(2)}, u32[]{:S(2)}) collective-permute-start(f32[7,10,1,256]{3,0,2,1:T(8,128)S(1)} %copy.53), channel_id=1, source_target_pairs={{0,1},{1,2},{2,3},{4,5},{5,6},{6,7},{8,9},{9,10},{10,11},{12,13},{... | collective-permute-start | bytes 215048 | tf_op jit(solution)/shard_map/ppermute | solution.py:20
  87.3 1.0 fusion.23
  88.9 5.3 %fusion.7 = f32[3,8,32,256]{3,2,1,0:T(8,128)} fusion(f32[3,8,32,256]{3,2,1,0:T(8,128)S(1)} %copy-done, f32[7,10,1,256]{3,2,1,0:T(1,128)S(1)} %copy.54, f32[7,1,32,256]{3,2,1,0:T(8,128)} %collective-permute-done, f32[7,1,32,256]{3,2,1,0:T(8,128)} %collective-permute-done.1, f32[1,8,32,256]{3,2,1,0:T(8,128)S(1)} %bitcast.63, ...), kind=kLoop, calls=%fused_computation.11 | loop fusion | flops 12582912 | bytes 8728576 | tf_op jit(solution)/shard_map/add | solution.py:70
  94.2 17.6 %copy.57 = f32[3,8,32,256]{0,3,2,1:T(8,128)} copy(f32[3,8,32,256]{3,2,1,0:T(8,128)} %fusion.7) | data formatting | bytes 1572864 | tf_op jit(solution)/shard_map/add | solution.py:70
  111.8 71.8 %scatter_fusion.1 = f32[3,65536]{0,1:T(8,128)} fusion(f32[3,65536]{0,1:T(8,128)} %bitcast.56, s32[8192]{0:T(1024)S(1)} %bitcast.64, f32[8192,3]{1,0:T(8,128)} %copy.60), kind=kCustom, calls=%fused_computation.2 | custom fusion | flops 24576 | bytes 327680 | tf_op jit(solution)/shard_map/scatter-add | solution.py:103
  183.5 13.2 %reduce_sum.9 = f32[3,16]{0,1:T(8,128)S(1)} reduce(f32[3,8,32,16,16]{0,4,3,2,1:T(8,128)} %bitcast.57, f32[]{:T(128)} %constant.132.clone.1), dimensions={1,2,4}, to_apply=%region_5.6 | reduce | flops 196560 | bytes 786628 | tf_op jit(solution)/shard_map/reduce_sum | solution.py:142
  196.8 41.2 %all-gather = f32[32,16,3]{1,2,0:T(4,128)S(1)} all-gather(f32[1,16,3]{1,2,0:T(4,128)S(1)} %bitcast.67), channel_id=1, replica_groups=mesh['slab'=8,'pencil'=4] {'slab','pencil'}, dimensions={0}, use_global_device_ids=true | all-gather | bytes 6336 | tf_op jit(solution)/shard_map/all_gather | solution.py:148
  239.4 20.2 %copy.63 = f32[3,8,32,256]{3,2,1,0:T(8,128)} copy(f32[3,8,32,256]{0,3,2,1:T(8,128)} %bitcast.58) | data formatting | bytes 1572864
  (55 shorter events, 8.6 us)
Async XLA Ops:
  0.6 88.2 %copy-start.2 = (f32[8,32,256]{2,1,0:T(8,128)S(1)}, f32[8,32,256]{2,1,0:T(8,128)}, u32[]{:S(2)}) copy-start(f32[8,32,256]{2,1,0:T(8,128)} %param.9) | copy-start | bytes 786436
  0.6 88.2 %copy-start = (f32[3,8,32,256]{3,2,1,0:T(8,128)S(1)}, f32[3,8,32,256]{3,2,1,0:T(8,128)}, u32[]{:S(2)}) copy-start(f32[3,8,32,256]{3,2,1,0:T(8,128)} %param.7) | copy-start | bytes 2359300
  0.7 88.2 %copy-start.1 = (f32[3,8,32,256]{3,2,1,0:T(8,128)S(1)}, f32[3,8,32,256]{3,2,1,0:T(8,128)}, u32[]{:S(2)}) copy-start(f32[3,8,32,256]{3,2,1,0:T(8,128)} %param.8) | copy-start | bytes 2359300
  2.7 77.8 %collective-permute-start = (f32[7,1,32,256]{3,2,1,0:T(8,128)}, f32[7,1,32,256]{3,2,1,0:T(8,128)}, u32[]{:S(2)}, u32[]{:S(2)}) collective-permute-start(f32[7,1,32,256]{3,2,1,0:T(8,128)} %get-tuple-element.17), channel_id=1, source_target_pairs={{4,0},{8,4},{12,8},{16,12},{20,16},{24,20},{28,24},{5,1},{9,5},{13... | collective-permute-start | bytes 688136 | tf_op jit(solution)/shard_map/ppermute | solution.py:21
  4.0 76.5 %collective-permute-start.1 = (f32[7,1,32,256]{3,2,1,0:T(8,128)}, f32[7,1,32,256]{3,2,1,0:T(8,128)}, u32[]{:S(2)}, u32[]{:S(2)}) collective-permute-start(f32[7,1,32,256]{3,2,1,0:T(8,128)} %get-tuple-element.16), channel_id=1, source_target_pairs={{0,4},{4,8},{8,12},{12,16},{16,20},{20,24},{24,28},{1,5},{5,9},{9,... | collective-permute-start | bytes 688136 | tf_op jit(solution)/shard_map/ppermute | solution.py:20
  51.7 0.8 copy-start.3
  79.2 32.5 %copy-start.4 = (s32[8192,1]{0,1:T(1,128)S(1)}, s32[8192,1]{0,1:T(1,128)}, u32[]{:S(2)}) copy-start(s32[8192,1]{0,1:T(1,128)} %compare_select_fusion.1) | copy-start | bytes 98308
  82.0 4.4 %collective-permute-start.2 = (f32[7,10,1,256]{3,0,2,1:T(8,128)S(1)}, f32[7,10,1,256]{3,0,2,1:T(8,128)S(1)}, u32[]{:S(2)}, u32[]{:S(2)}) collective-permute-start(f32[7,10,1,256]{3,0,2,1:T(8,128)S(1)} %copy.51), channel_id=1, source_target_pairs={{1,0},{2,1},{3,2},{5,4},{6,5},{7,6},{9,8},{10,9},{11,10},{13,12},{... | collective-permute-start | bytes 215048 | tf_op jit(solution)/shard_map/ppermute | solution.py:21
  83.3 3.9 %collective-permute-start.3 = (f32[7,10,1,256]{3,0,2,1:T(8,128)S(1)}, f32[7,10,1,256]{3,0,2,1:T(8,128)S(1)}, u32[]{:S(2)}, u32[]{:S(2)}) collective-permute-start(f32[7,10,1,256]{3,0,2,1:T(8,128)S(1)} %copy.53), channel_id=1, source_target_pairs={{0,1},{1,2},{2,3},{4,5},{5,6},{6,7},{8,9},{9,10},{10,11},{12,13},{... | collective-permute-start | bytes 215048 | tf_op jit(solution)/shard_map/ppermute | solution.py:20
  94.2 143.9 %copy-start.5 = (f32[512]{0:T(512)S(1)}, f32[512]{0:T(512)}, u32[]{:S(2)}) copy-start(f32[512]{0:T(512)} %get-tuple-element.48) | copy-start | bytes 6148
  94.2 143.9 %copy-start.6 = (f32[512]{0:T(512)S(1)}, f32[512]{0:T(512)}, u32[]{:S(2)}) copy-start(f32[512]{0:T(512)} %get-tuple-element.49) | copy-start | bytes 6148
  94.2 143.9 %copy-start.7 = (f32[512]{0:T(512)S(1)}, f32[512]{0:T(512)}, u32[]{:S(2)}) copy-start(f32[512]{0:T(512)} %fusion.77) | copy-start | bytes 6148
where the time goes:
time: 262 us; the launch traced here: 260 us
  other arithmetic  104 us (40%)
  blocking collectives  73.4 us (28%)
  local copies, waits for them, and re-layouts  67.8 us (26%)
  starting transfers between devices  11.8 us (5%)
    scatter-add x1, other arithmetic, deposit(): return field_flat.at[:, local_cells.reshape(-1)].add(values)  71.8 us
    all_gather x1, blocking collectives, per_device(): piece = lax.all_gather(moment, ('slab', 'pencil'), axis=1, tiled=True)  41.2 us
    all_gather x1, blocking collectives, per_device(): arrived = lax.all_gather(payload, 'slab', axis=0, tiled=True)  32.2 us
    unnamed x20, local copies, waits for them, and re-layouts  21.8 us
    add x1, local copies, waits for them, and re-layouts, advance(): return own_vort + time_step * (stretch + diffuse)  17.6 us
    scatter x1, local copies, waits for them, and re-layouts, per_device(): compact_weights = jnp.zeros((rows_kept, 3, tile_len), jnp.float32).at[pos...  15.1 us
    reduce_sum x1, other arithmetic, per_device(): vorticity_out.reshape(3, cx_dev, cy_dev, NCL, CB).sum(axis=(1, 2, 4))  13.2 us
    ppermute x2, starting transfers between devices, with_halo(): before = lax.ppermute(last, axis, up)  9.2 us
  transfers between devices with their start and end apart: 4, of which 1 were waited for; matrix products, arithmetic and copies ran while one was open for 14% of the time, Pallas kernels for 0%

commit v1 on v0

v1 whole, which is shorter than its diff:
```python
import functools

import jax
import jax.numpy as jnp
from jax import lax
from jax.experimental import pallas as pl
from jax.experimental.pallas import tpu as pltpu
from jax.sharding import PartitionSpec as P

CB = 16
TIME_STEP = 0.1
LANES = 128
GROUP = 4
VMEM_LIMIT = 48 * 1024 * 1024

VMEM = pl.BlockSpec(memory_space=pltpu.VMEM)
SMEM = pl.BlockSpec(memory_space=pltpu.SMEM)
PARAMS = pltpu.CompilerParams(vmem_limit_bytes=VMEM_LIMIT)


def shaped(*shape):
    return jax.ShapeDtypeStruct(shape, jnp.float32)


def pack_kernel(cap, vort, velo, visc, weights, cells, dest, count, xlo, xhi, ylo, yhi, packets, filled):
    cx, cy = visc.shape[0], visc.shape[1]
    for face, at in ((xlo, 0), (xhi, cx - 1)):
        face[0:3] = vort[:, at]
        face[3:6] = velo[:, at]
        face[6] = visc[at]
    for face, at in ((ylo, 0), (yhi, cy - 1)):
        for x in range(cx):
            for c in range(3):
                face[c, x : x + 1, :] = vort[c, x, at : at + 1, :]
                face[3 + c, x : x + 1, :] = velo[c, x, at : at + 1, :]
            face[6, x : x + 1, :] = visc[x, at : at + 1, :]
    packets[...] = jnp.zeros_like(packets)
    n_slab = packets.shape[0] // cap
    for d in range(n_slab):
        filled[d] = 0

    def place(r, carry):
        d = dest[r, 0]
        slot = filled[d]
        at = d * cap + slot
        packets[at, 0:3, :] = weights[r]
        packets[at, 3:4, :] = cells[pl.ds(r, 1), :].astype(jnp.float32)
        filled[d] = slot + 1
        return carry

    lax.fori_loop(0, count[0], place, 0)


def pack(vort, velo, visc, weights, cells, dest, count, n_slab):
    _, cx, cy, nz = vort.shape
    cap = 2 * weights.shape[0] // n_slab
    return pl.pallas_call(
        functools.partial(pack_kernel, cap),
        out_shape=(
            shaped(7, cy, nz),
            shaped(7, cy, nz),
            shaped(7, cx, nz),
            shaped(7, cx, nz),
            shaped(n_slab * cap, 4, weights.shape[2]),
        ),
        in_specs=[VMEM] * 5 + [SMEM] * 2,
        out_specs=(VMEM,) * 5,
        scratch_shapes=[pltpu.SMEM((n_slab,), jnp.int32)],
        compiler_params=PARAMS,
    )(vort, velo, visc, weights, cells, dest, count)


def ahead(a, axis):
    return pltpu.roll(a, a.shape[axis] - 1, axis)


def behind(a, axis):
    return pltpu.roll(a, 1, axis)


def interior_step(vort, velo, visc, out):
    cx, cy, nz = visc.shape
    row = lax.broadcasted_iota(jnp.int32, (cy, nz), 0)
    has_ahead = row < cy - 1
    has_behind = row > 0
    for x in range(cx):
        nu = visc[x]
        spin = [vort[c, x] for c in range(3)]
        mean_y = jnp.where(has_ahead, 0.5 * (nu + ahead(nu, 0)), 0.0)
        mean_z = 0.5 * (nu + ahead(nu, 1))
        if x < cx - 1:
            mean_next = 0.5 * (nu + visc[x + 1])
        if x > 0:
            mean_last = 0.5 * (nu + visc[x - 1])
        for c in range(3):
            w = spin[c]
            u = velo[c, x]
            flux_y = mean_y * (ahead(w, 0) - w)
            flux_z = mean_z * (ahead(w, 1) - w)
            change = (flux_y - behind(flux_y, 0)) + (flux_z - behind(flux_z, 1))
            slope_y = jnp.where(has_ahead, ahead(u, 0), 0.0) - jnp.where(has_behind, behind(u, 0), 0.0)
            slope_z = ahead(u, 1) - behind(u, 1)
            if x == 0:
                slope_x = velo[c, x + 1]
            elif x == cx - 1:
                slope_x = -velo[c, x - 1]
            else:
                slope_x = velo[c, x + 1] - velo[c, x - 1]
            stretch = 0.5 * (spin[0] * slope_x + spin[1] * slope_y + spin[2] * slope_z)
            if x < cx - 1:
                change = change + mean_next * (vort[c, x + 1] - w)
            if x > 0:
                change = change + mean_last * (vort[c, x - 1] - w)
            out[c, x] = w + TIME_STEP * (stretch + change)


def deposit(packets, out):
    _, cx, cy, nz = out.shape
    rows = cx * cy
    wide = GROUP * packets.shape[2]
    row_iota = lax.broadcasted_iota(jnp.int32, (rows, wide), 0)
    col_iota = row_iota if nz == rows else lax.broadcasted_iota(jnp.int32, (nz, wide), 0)

    def group(g, carry):
        tiles = [packets[g * GROUP + k] for k in range(GROUP)]
        block = jnp.concatenate(tiles, axis=1)
        cell = block[3:4, :].astype(jnp.int32)
        at_row = row_iota == cell // nz
        at_col = col_iota == cell % nz
        spots = at_col.astype(jnp.float32).astype(jnp.bfloat16)
        parts = []
        for c in range(3):
            w = block[c : c + 1, :]
            high = w.astype(jnp.bfloat16).astype(jnp.float32)
            low = w - high
            parts.append(
                jnp.concatenate(
                    [jnp.where(at_row, piece, 0.0).astype(jnp.bfloat16) for piece in (high, low)], axis=1
                )
            )
        left = jnp.concatenate(parts, axis=0)
        right = jnp.concatenate([spots, spots], axis=1)
        added = lax.dot_general(
            left, right, (((1,), (1,)), ((), ())), preferred_element_type=jnp.float32
        )
        out[...] += added.reshape(out.shape)
        return carry

    lax.fori_loop(0, packets.shape[0] // GROUP, group, 0)


def inner_kernel(vort, velo, visc, packets, out, sums):
    interior_step(vort, velo, visc, out)
    deposit(packets, out)
    for c in range(3):
        sums[c : c + 1, :] = jnp.sum(out[c].reshape(-1, out.shape[3]), axis=0, keepdims=True)


def inner(vort, velo, visc, packets):
    return pl.pallas_call(
        inner_kernel,
        out_shape=(shaped(*vort.shape), shaped(3, vort.shape[3])),
        in_specs=[VMEM] * 4,
        out_specs=(VMEM,) * 2,
        compiler_params=PARAMS,
    )(vort, velo, visc, packets)


def face_change(own, other, along, sign, c):
    stretch = (0.5 * sign) * own[along] * other[3 + c]
    diffuse = 0.5 * (own[6] + other[6]) * (other[c] - own[c])
    return TIME_STEP * (stretch + diffuse)


def edge_kernel(inside, sums, xlo, xhi, ylo, yhi, xlo_in, xhi_in, ylo_in, yhi_in, out, moments):
    _, cx, cy, nz = out.shape
    out[...] = inside[...]
    row = lax.broadcasted_iota(jnp.int32, (nz, LANES), 0)
    lane = lax.broadcasted_iota(jnp.int32, (nz, LANES), 1)
    packed = jnp.zeros((1, LANES), jnp.float32)
    for c in range(3):
        total = sums[c : c + 1, :]
        for own, other, at, sign in ((xlo, xlo_in, 0, -1.0), (xhi, xhi_in, cx - 1, 1.0)):
            change = face_change(own, other, 0, sign, c)
            out[c, at] = out[c, at] + change
            total = total + jnp.sum(change, axis=0, keepdims=True)
        for own, other, at, sign in ((ylo, ylo_in, 0, -1.0), (yhi, yhi_in, cy - 1, 1.0)):
            change = face_change(own, other, 1, sign, c)
            for x in range(cx):
                out[c, x, at : at + 1, :] = out[c, x, at : at + 1, :] + change[x : x + 1, :]
            total = total + jnp.sum(change, axis=0, keepdims=True)
        gather = (lane == row // CB + c * (nz // CB)).astype(jnp.float32)
        packed = packed + jnp.dot(total, gather, precision=lax.Precision.HIGHEST, preferred_element_type=jnp.float32)
    for k in range(moments.shape[0]):
        moments[k] = packed


def edges(inside, sums, faces, halos, n_all):
    return pl.pallas_call(
        edge_kernel,
        out_shape=(shaped(*inside.shape), shaped(n_all, 1, LANES)),
        in_specs=[VMEM] * 10,
        out_specs=(VMEM,) * 2,
        compiler_params=PARAMS,
    )(inside, sums, *faces, *halos)


def far_kernel(cx, cy, ncl, n_slab, n_pencil, moments, out):
    n_all = n_slab * n_pencil
    shape = (n_all, LANES)
    slab = lax.axis_index("slab")
    pencil = lax.axis_index("pencil")
    source = lax.broadcasted_iota(jnp.int32, shape, 0)
    lane = lax.broadcasted_iota(jnp.int32, shape, 1)
    level = lane % ncl
    sigma = jnp.float32(cx * n_slab // 4)
    rel_x = ((slab - source // n_pencil) * cx).astype(jnp.float32)
    rel_y = ((pencil - source % n_pencil) * cy).astype(jnp.float32)
    flat = rel_x * rel_x + rel_y * rel_y
    moment = moments[...].reshape(shape)
    along = ([], [], [])
    for i in range(ncl):
        rel_z = ((i - level) * CB).astype(jnp.float32)
        inverse = lax.rsqrt(flat + rel_z * rel_z + sigma * sigma)
        weighted = (inverse * inverse * inverse) * moment
        for rows, rel in zip(along, (rel_x, rel_y, rel_z)):
            rows.append(jnp.sum(rel * weighted, axis=0, keepdims=True))
    part = lax.broadcasted_iota(jnp.int32, (8, LANES), 0)
    pick = (lax.broadcasted_iota(jnp.int32, (8, LANES), 1) // ncl == part).astype(jnp.float32)
    by_x, by_y, by_z = [
        lax.dot_general(
            pick,
            jnp.concatenate(rows, axis=0),
            (((1,), (1,)), ((), ())),
            precision=lax.Precision.HIGHEST,
            preferred_element_type=jnp.float32,
        )
        for rows in along
    ]
    out[0, 0] = by_z[1:2] - by_y[2:3]
    out[1, 0] = by_x[2:3] - by_z[0:1]
    out[2, 0] = by_y[0:1] - by_x[1:2]


def far(moments, cx, cy, ncl, n_slab, n_pencil):
    return pl.pallas_call(
        functools.partial(far_kernel, cx, cy, ncl, n_slab, n_pencil),
        out_shape=shaped(3, 1, 1, ncl),
        in_specs=[VMEM],
        out_specs=VMEM,
        compiler_params=PARAMS,
    )(moments)


def shift(array, axis, step):
    n = lax.axis_size(axis)
    pairs = [(i, i + step) for i in range(n) if 0 <= i + step < n]
    return lax.ppermute(array, axis, pairs)


def per_device(vorticity, velocity, viscosity, tile_weights, tile_cells, tile_dest, tile_count):
    _, cx, cy, nz = vorticity.shape
    n_slab = lax.axis_size("slab")
    n_pencil = lax.axis_size("pencil")
    n_all = n_slab * n_pencil
    xlo, xhi, ylo, yhi, packets = pack(
        vorticity, velocity, viscosity, tile_weights, tile_cells, tile_dest, tile_count, n_slab
    )
    arrived = lax.all_to_all(packets, "slab", 0, 0, tiled=True)
    xlo_in = shift(xhi, "slab", 1)
    xhi_in = shift(xlo, "slab", -1)
    ylo_in = shift(yhi, "pencil", 1)
    yhi_in = shift(ylo, "pencil", -1)
    inside, sums = inner(vorticity, velocity, viscosity, arrived)
    vorticity_out, moments = edges(
        inside, sums, (xlo, xhi, ylo, yhi), (xlo_in, xhi_in, ylo_in, yhi_in), n_all
    )
    gathered = lax.all_to_all(moments, ("slab", "pencil"), 0, 0, tiled=True)
    far_velocity = far(gathered, cx, cy, nz // CB, n_slab, n_pencil)
    return (vorticity_out, far_velocity)


def solution(mesh):
    in_specs = (
        P(None, "slab", "pencil", None),
        P(None, "slab", "pencil", None),
        P("slab", "pencil", None),
        P(("slab", "pencil"), None, None),
        P(("slab", "pencil"), None),
        P(("slab", "pencil"), None),
        P(("slab", "pencil")),
    )
    out_specs = (P(None, "slab", "pencil", None), P(None, "slab", "pencil", None))
    return jax.shard_map(
        per_device, mesh=mesh, in_specs=in_specs, out_specs=out_specs, check_vma=False
    )
```

time: 262 us -> 52.9 us (0.20)
  other arithmetic: 104 us -> 0 us
  local copies, waits for them, and re-layouts: 67.8 us -> 4.17 us
  blocking collectives: 73.4 us -> 13 us
  Pallas kernels: 0 us -> 16.2 us
  starting transfers between devices: 11.8 us -> 17.7 us
    all_gather x2 -> x0, blocking collectives: 73.4 us -> none  [the longest x1 41.2 us: per_device(): piece = lax.all_gather(moment, ('slab', 'pencil'), axis=1, tiled=True)]
    scatter-add x1 -> x0, other arithmetic: 71.8 us -> none  [deposit(): return field_flat.at[:, local_cells.reshape(-1)].add(values)]
    unnamed x20 -> x18, local copies, waits for them, and re-layouts: 21.8 us -> 4.17 us
    add x1 -> x0, local copies, waits for them, and re-layouts: 17.6 us -> none  [advance(): return own_vort + time_step * (stretch + diffuse)]
    pallas_call x0 -> x4, Pallas kernels: none -> 16.2 us  [the longest x1 12.4 us: inner(): pl.pallas_call(inner_kernel, out_shape=(shaped(*vort.shape), shaped(3, vo...]
    scatter x1 -> x0, local copies, waits for them, and re-layouts: 15.1 us -> none  [per_device(): compact_weights = jnp.zeros((rows_kept, 3, tile_len), jnp.float32).at[pos...]
    reduce_sum x1 -> x0, other arithmetic: 13.2 us -> none  [per_device(): vorticity_out.reshape(3, cx_dev, cy_dev, NCL, CB).sum(axis=(1, 2, 4))]
    all_to_all x0 -> x1, blocking collectives: none -> 13 us  [per_device(): gathered = lax.all_to_all(moments, ('slab', 'pencil'), 0, 0, tiled=True)]
  transfers between devices with their start and end apart: 4 -> 5, of which waited for: 1 -> 0; matrix products, arithmetic and copies ran while one was open for 14% -> 0% of each run, Pallas kernels for 0% -> 24%
where the time goes in v1:
time: 52.9 us; the launch traced here: 52.5 us
  starting transfers between devices  17.7 us (33%)
  Pallas kernels  16.2 us (31%)
  blocking collectives  13 us (25%)
  local copies, waits for them, and re-layouts  4.17 us (8%)
  between operations  1.43 us (3%)
    all_to_all x1, blocking collectives, per_device(): gathered = lax.all_to_all(moments, ('slab', 'pencil'), 0, 0, tiled=True)  13 us
    pallas_call x1, Pallas kernels, inner(): pl.pallas_call(inner_kernel, out_shape=(shaped(*vort.shape), shaped(3, vo...  12.4 us
    ppermute x4, starting transfers between devices, shift(): return lax.ppermute(array, axis, pairs)  10.2 us
    all_to_all x1, starting transfers between devices, per_device(): arrived = lax.all_to_all(packets, 'slab', 0, 0, tiled=True)  7.51 us
    unnamed x18, local copies, waits for them, and re-layouts  4.17 us
    pallas_call x1, Pallas kernels, pack(): pl.pallas_call(functools.partial(pack_kernel, cap), out_shape=(shaped(7,...  1.67 us
    pallas_call x1, Pallas kernels, edges(): pl.pallas_call(edge_kernel, out_shape=(shaped(*inside.shape), shaped(n_al...  1.24 us
  transfers between devices with their start and end apart: 5, of which 0 were waited for; matrix products, arithmetic and copies ran while one was open for 0% of the time, Pallas kernels for 24%

profile of v1, /device:TPU:0, one launch (start us, length us, event | category | flops | bytes accessed | tf_op | source)
XLA Modules:
  0.0 52.5 jit_solution(17331330989135071633)
XLA Ops:
  0.6 0.0 copy-start.7
  1.3 0.0 copy-done.7
  1.3 0.1 copy.10.dest
  1.4 0.8 %copy.9.weights = f32[32,3,128]{2,1,0:T(4,128)S(1)} copy(f32[32,3,128]{2,0,1:T(8,128)} %param.10) | data formatting | bytes 98304 | tf_op args[3]
  2.2 0.0 copy-done.6
  2.3 0.0 copy-start
  2.3 1.1 %copy-done = f32[3,8,32,256]{3,2,1,0:T(8,128)S(1)} copy-done((f32[3,8,32,256]{3,2,1,0:T(8,128)S(1)}, f32[3,8,32,256]{3,2,1,0:T(8,128)}, u32[]{:S(2)}) %copy-start) | copy-done | bytes 786456
  3.4 1.1 %copy-done.2 = f32[3,8,32,256]{3,2,1,0:T(8,128)S(1)} copy-done((f32[3,8,32,256]{3,2,1,0:T(8,128)S(1)}, f32[3,8,32,256]{3,2,1,0:T(8,128)}, u32[]{:S(2)}) %copy-start.2) | copy-done | bytes 786456
  4.5 0.9 %copy-done.4 = f32[8,32,256]{2,1,0:T(8,128)S(1)} copy-done((f32[8,32,256]{2,1,0:T(8,128)S(1)}, f32[8,32,256]{2,1,0:T(8,128)}, u32[]{:S(2)}) %copy-start.4) | copy-done | bytes 262168
  5.5 1.7 %shard_map.86 = (f32[7,32,256]{2,1,0:T(8,128)S(1)}, f32[7,32,256]{2,1,0:T(8,128)S(1)}, f32[7,8,256]{2,1,0:T(8,128)S(1)}, f32[7,8,256]{2,1,0:T(8,128)S(1)}, f32[64,4,128]{2,1,0:T(4,128)}) custom-call(f32[3,8,32,256]{3,2,1,0:T(8,128)S(1)} %copy-done, f32[3,8,32,256]{3,2,1,0:T(8,128)S(1)} %copy-done.2, f32[8,32,256]{2,1,0:T(8,128)S(1)} %copy-done.4, ...), custom_call_target="tpu_custom_call" | custom-call | tf_op jit(solution)/shard_map/pallas_call | solution.py:57
  7.2 7.5 %all-to-all-start = ((f32[64,4,128]{2,1,0:T(4,128)}), f32[64,4,128]{2,1,0:T(4,128)S(1)}, u32[]{:S(2)}, u32[]{:S(2)}) async-start(f32[64,4,128]{2,1,0:T(4,128)} %get-tuple-element.11), calls=%async_computation | async-start | bytes 262144 | tf_op jit(solution)/shard_map/all_to_all | solution.py:269
  14.7 1.3 %collective-permute-start.1 = (f32[7,32,256]{2,1,0:T(8,128)S(1)}, f32[7,32,256]{2,1,0:T(8,128)S(1)}, u32[]{:S(2)}, u32[]{:S(2)}) collective-permute-start(f32[7,32,256]{2,1,0:T(8,128)S(1)} %get-tuple-element.14.xlo), channel_id=1, source_target_pairs={{4,0},{8,4},{12,8},{16,12},{20,16},{24,20},{28,24},{5,1},{9,5},{13... | collective-permute-start | bytes 688136 | tf_op jit(solution)/shard_map/ppermute | solution.py:258
  16.0 4.6 %collective-permute-start = (f32[7,32,256]{2,1,0:T(8,128)S(1)}, f32[7,32,256]{2,1,0:T(8,128)S(1)}, u32[]{:S(2)}, u32[]{:S(2)}) collective-permute-start(f32[7,32,256]{2,1,0:T(8,128)S(1)} %get-tuple-element.15.xhi), channel_id=1, source_target_pairs={{0,4},{4,8},{8,12},{12,16},{16,20},{20,24},{24,28},{1,5},{5,9},{9,... | collective-permute-start | bytes 688136 | tf_op jit(solution)/shard_map/ppermute | solution.py:258
  20.5 1.3 %collective-permute-start.3 = (f32[7,8,256]{2,1,0:T(8,128)S(1)}, f32[7,8,256]{2,1,0:T(8,128)S(1)}, u32[]{:S(2)}, u32[]{:S(2)}) collective-permute-start(f32[7,8,256]{2,1,0:T(8,128)S(1)} %get-tuple-element.16.ylo), channel_id=1, source_target_pairs={{1,0},{2,1},{3,2},{5,4},{6,5},{7,6},{9,8},{10,9},{11,10},{13,12},{... | collective-permute-start | bytes 172040 | tf_op jit(solution)/shard_map/ppermute | solution.py:258
  21.8 3.0 %collective-permute-start.2 = (f32[7,8,256]{2,1,0:T(8,128)S(1)}, f32[7,8,256]{2,1,0:T(8,128)S(1)}, u32[]{:S(2)}, u32[]{:S(2)}) collective-permute-start(f32[7,8,256]{2,1,0:T(8,128)S(1)} %get-tuple-element.17.yhi), channel_id=1, source_target_pairs={{0,1},{1,2},{2,3},{4,5},{5,6},{6,7},{8,9},{9,10},{10,11},{12,13},{... | collective-permute-start | bytes 172040 | tf_op jit(solution)/shard_map/ppermute | solution.py:258
  24.9 0.0 all-to-all-done.packets
  24.9 12.4 %shard_map.87 = (f32[3,8,32,256]{3,2,1,0:T(8,128)S(1)}, f32[3,256]{1,0:T(4,128)S(1)}) custom-call(f32[3,8,32,256]{3,2,1,0:T(8,128)S(1)} %copy-done.1, f32[3,8,32,256]{3,2,1,0:T(8,128)S(1)} %copy-done.3, f32[8,32,256]{2,1,0:T(8,128)S(1)} %copy-done.5, f32[64,4,128]{2,1,0:T(4,128)S(1)} %all-to-all-done.packets), custom_call_target="tpu_custom_call" | custom-call | tf_op jit(solution)/shard_map/pallas_call | solution.py:160
  37.3 0.0 collective-permute-done.3.yhi_in
  37.3 0.0 collective-permute-done.2.ylo_in
  37.3 0.0 collective-permute-done.1.xhi_in
  37.3 0.0 collective-permute-done.xlo_in
  37.4 1.2 %shard_map.88 = (f32[3,8,32,256]{3,2,1,0:T(8,128)}, f32[32,1,128]{2,1,0:T(1,128)S(1)}) custom-call(f32[3,8,32,256]{3,2,1,0:T(8,128)S(1)} %get-tuple-element.12.inside, f32[3,256]{1,0:T(4,128)S(1)} %get-tuple-element.13.sums, f32[7,32,256]{2,1,0:T(8,128)S(1)} %get-tuple-element.14.xlo, f32[7,32,256]{2,1,0:T(8,128)S(1)} %get-tuple-element.15.xhi, ...), custom_call_target="tpu_custom_call" | custom-call | tf_op jit(solution)/shard_map/pallas_call | solution.py:199
  38.6 13.0 %all_to_all.10.moments = f32[32,1,128]{2,1,0:T(1,128)S(1)} all-to-all(f32[32,1,128]{2,1,0:T(1,128)S(1)} %get-tuple-element.19), channel_id=1, replica_groups=mesh['slab'=8,'pencil'=4] {'slab','pencil'}, dimensions={0} | all-to-all | bytes 32768 | tf_op jit(solution)/shard_map/all_to_all | solution.py:278
  51.6 0.9 %shard_map.89 = f32[3,1,1,16]{3,2,1,0:T(1,128)} custom-call(f32[32,1,128]{2,1,0:T(1,128)S(1)} %all_to_all.10.moments), custom_call_target="tpu_custom_call" | custom-call | tf_op jit(solution)/shard_map/pallas_call | solution.py:246
  (9 shorter events, 0.0 us)
Async XLA Ops:
  0.6 0.7 %copy-start.7 = (s32[32,1]{0,1:T(1,128)S(1)}, s32[32,1]{0,1:T(1,128)}, u32[]{:S(2)}) copy-start(s32[32,1]{0,1:T(1,128)} %param.12) | copy-start | bytes 388
  1.4 0.9 %copy-start.6 = (s32[32,128]{1,0:T(8,128)S(1)}, s32[32,128]{1,0:T(8,128)}, u32[]{:S(2)}) copy-start(s32[32,128]{1,0:T(8,128)} %cells.1) | copy-start | bytes 49156
  2.3 1.1 %copy-start = (f32[3,8,32,256]{3,2,1,0:T(8,128)S(1)}, f32[3,8,32,256]{3,2,1,0:T(8,128)}, u32[]{:S(2)}) copy-start(f32[3,8,32,256]{3,2,1,0:T(8,128)} %vort.3) | copy-start | bytes 2359300
  3.4 1.1 %copy-start.2 = (f32[3,8,32,256]{3,2,1,0:T(8,128)S(1)}, f32[3,8,32,256]{3,2,1,0:T(8,128)}, u32[]{:S(2)}) copy-start(f32[3,8,32,256]{3,2,1,0:T(8,128)} %velo.3) | copy-start | bytes 2359300
  4.5 0.9 %copy-start.4 = (f32[8,32,256]{2,1,0:T(8,128)S(1)}, f32[8,32,256]{2,1,0:T(8,128)}, u32[]{:S(2)}) copy-start(f32[8,32,256]{2,1,0:T(8,128)} %visc.3) | copy-start | bytes 786436
  5.5 19.4 %copy-start.1 = (f32[3,8,32,256]{3,2,1,0:T(8,128)S(1)}, f32[3,8,32,256]{3,2,1,0:T(8,128)}, u32[]{:S(2)}) copy-start(f32[3,8,32,256]{3,2,1,0:T(8,128)} %vort.3) | copy-start | bytes 2359300
  5.5 19.4 %copy-start.3 = (f32[3,8,32,256]{3,2,1,0:T(8,128)S(1)}, f32[3,8,32,256]{3,2,1,0:T(8,128)}, u32[]{:S(2)}) copy-start(f32[3,8,32,256]{3,2,1,0:T(8,128)} %velo.3) | copy-start | bytes 2359300
  7.2 17.7 %copy-start.5 = (f32[8,32,256]{2,1,0:T(8,128)S(1)}, f32[8,32,256]{2,1,0:T(8,128)}, u32[]{:S(2)}) copy-start(f32[8,32,256]{2,1,0:T(8,128)} %visc.3) | copy-start | bytes 786436
  7.2 17.7 %all-to-all-start = ((f32[64,4,128]{2,1,0:T(4,128)}), f32[64,4,128]{2,1,0:T(4,128)S(1)}, u32[]{:S(2)}, u32[]{:S(2)}) async-start(f32[64,4,128]{2,1,0:T(4,128)} %get-tuple-element.11), calls=%async_computation | async-start | bytes 262144 | tf_op jit(solution)/shard_map/all_to_all | solution.py:269
  14.7 22.7 %collective-permute-start.1 = (f32[7,32,256]{2,1,0:T(8,128)S(1)}, f32[7,32,256]{2,1,0:T(8,128)S(1)}, u32[]{:S(2)}, u32[]{:S(2)}) collective-permute-start(f32[7,32,256]{2,1,0:T(8,128)S(1)} %get-tuple-element.14.xlo), channel_id=1, source_target_pairs={{4,0},{8,4},{12,8},{16,12},{20,16},{24,20},{28,24},{5,1},{9,5},{13... | collective-permute-start | bytes 688136 | tf_op jit(solution)/shard_map/ppermute | solution.py:258
  16.0 21.4 %collective-permute-start = (f32[7,32,256]{2,1,0:T(8,128)S(1)}, f32[7,32,256]{2,1,0:T(8,128)S(1)}, u32[]{:S(2)}, u32[]{:S(2)}) collective-permute-start(f32[7,32,256]{2,1,0:T(8,128)S(1)} %get-tuple-element.15.xhi), channel_id=1, source_target_pairs={{0,4},{4,8},{8,12},{12,16},{16,20},{20,24},{24,28},{1,5},{5,9},{9,... | collective-permute-start | bytes 688136 | tf_op jit(solution)/shard_map/ppermute | solution.py:258
  20.5 16.8 %collective-permute-start.3 = (f32[7,8,256]{2,1,0:T(8,128)S(1)}, f32[7,8,256]{2,1,0:T(8,128)S(1)}, u32[]{:S(2)}, u32[]{:S(2)}) collective-permute-start(f32[7,8,256]{2,1,0:T(8,128)S(1)} %get-tuple-element.16.ylo), channel_id=1, source_target_pairs={{1,0},{2,1},{3,2},{5,4},{6,5},{7,6},{9,8},{10,9},{11,10},{13,12},{... | collective-permute-start | bytes 172040 | tf_op jit(solution)/shard_map/ppermute | solution.py:258
  21.8 15.5 %collective-permute-start.2 = (f32[7,8,256]{2,1,0:T(8,128)S(1)}, f32[7,8,256]{2,1,0:T(8,128)S(1)}, u32[]{:S(2)}, u32[]{:S(2)}) collective-permute-start(f32[7,8,256]{2,1,0:T(8,128)S(1)} %get-tuple-element.17.yhi), channel_id=1, source_target_pairs={{0,1},{1,2},{2,3},{4,5},{5,6},{6,7},{8,9},{9,10},{10,11},{12,13},{... | collective-permute-start | bytes 172040 | tf_op jit(solution)/shard_map/ppermute | solution.py:258
